TPU v7x, 256 devices: a whole 4x4x8 slice. The times are simulated.
256 devices in a mesh: coil: 8 (over x, core), tile: 32 (over z, y).
Axes of the slice: x: 4, y: 4, z: 8, core: 2. Of those that a mesh axis runs over, the one named last changes fastest.
Arguments:
- image_p: float32 [2, 128, 128, 128], P(None, 'tile', 'coil'), may hold values from -6 to 6
- image_x: float32 [2, 128, 128, 128], P(None, 'tile', 'coil'), may hold values from -6 to 6
- image_r: float32 [2, 128, 128, 128], P(None, 'tile', 'coil'), may hold values from -6 to 6
- sensitivity: float32 [8, 2, 128, 128, 128], P('coil', None, 'tile'), may hold values from -5 to 5
- kb_weights: float32 [1024, 3, 4, 128], P('tile'), may hold values from -3 to 3
- block_owner: int32 [1024], P('tile'), may hold values from 0 to 31, as said below
- owner_list: int32 [3, 32, 32, 4], P(None, 'tile'), may hold values from -1 to 124, as said below
Outputs:
- next_x: float32 [2, 128, 128, 128], P(None, 'tile', 'coil')
- next_r: float32 [2, 128, 128, 128], P(None, 'tile', 'coil')
- next_p: float32 [2, 128, 128, 128], P(None, 'tile', 'coil')
Inputs may be any that keep to these rules, and one draw needn't show every extreme that they name: `block_owner`: of the 32 blocks handled by one index of tile (blocks h * 32 to h * 32 + 31), at most 4 have any one owner; in every draw each such device has exactly 4 blocks of one common owner. owner_list[:, o, h, k] holds the offsets (kx, ky within tile o, kz) of the block of rank k among the blocks of device h whose owner is o, in the order of their slots; all three are -1 where there is no such block. Offsets place the whole box inside the grid and inside tile o.
All inputs are finite; a program needn't handle non-finite values.
Results may differ from a plain program's by a relative error of at most 0.0002.
Values sent between devices are 32-bit elements; how exact they have to be, the bound alone decides.
A program may use at most 128 MiB of HBM per device.

v0:
```python
import functools
import math

import jax
import jax.numpy as jnp
import ml_dtypes
import numpy as np
from jax import lax
from jax.experimental import pallas as pl
from jax.experimental.pallas import tpu as pltpu
from jax.sharding import PartitionSpec as P

N = 128
NC = 8
NT = 32
CAP = 4
SLOTS = 32
F32, BF16, I32 = jnp.float32, jnp.bfloat16, jnp.int32
MESH = pl.DeviceIdType.MESH
ANY = pl.BlockSpec(memory_space=pl.ANY)
SMEM = pl.BlockSpec(memory_space=pltpu.SMEM)


def tables():
    cells = np.arange(N)
    angle = 2.0 * math.pi / N * ((cells[:, None] * cells[None, :]) % N)
    cos, sin = np.cos(angle) / math.sqrt(N), np.sin(angle) / math.sqrt(N)
    left = np.block([[cos, sin], [-sin, cos]])
    order = [c * N + 4 * t + i for t in range(NT) for c in range(2) for i in range(4)]
    out = []
    for table in (left, left.T, left[:, order], left[:, order].T):
        table = table.astype(np.float32)
        high = table.astype(ml_dtypes.bfloat16)
        low = (table - high.astype(np.float32)).astype(ml_dtypes.bfloat16)
        out += [high, low]
    return np.stack(out)


def split(x):
    high = x.astype(BF16)
    return high, (x - high.astype(F32)).astype(BF16)


def dot(a, b):
    return jnp.dot(a, b, preferred_element_type=F32)


def dot3(a, b):
    return dot(a[0], b[0]) + (dot(a[0], b[1]) + dot(a[1], b[0]))


def kernel(
    p_hbm, x_hbm, r_hbm, s_hbm, kb_hbm, own, offs, tab_hbm,
    ox_hbm, or_hbm, op_hbm,
    tab, smap, kb, xv, rv, pbuf, wsend, wbuf, onehot, pt, pi,
    send1, recv1, boxes, placed, gacc, send2, recv2, rs_send, rs_recv,
    nx, nr, npv, ar1, ar1c, ar1t, ar2, ar2c, ar2t,
    load_sem, loc_sem, ag_s, ag_r, w1_s, w1_r, w2_s, w2_r, a1_s, a1_r, a2_s, a2_r,
    rs_s, rs_r, r1c_s, r1c_r, r1t_s, r1t_r, r2c_s, r2c_r, r2t_s, r2t_r, out_sem,
):
    ci, ti = lax.axis_index("coil"), lax.axis_index("tile")

    loads = [
        pltpu.make_async_copy(src, dst, load_sem.at[i])
        for i, (src, dst) in enumerate(
            [
                (kb_hbm, kb),
                (tab_hbm, tab),
                (s_hbm.at[0], smap),
                (p_hbm, pbuf.at[ci]),
                (x_hbm, xv),
                (r_hbm, rv),
            ]
        )
    ]
    for load in loads:
        load.start()

    def others(size, me, body):
        def step(s, carry):
            body(lax.rem(me + s, size))
            return carry

        lax.fori_loop(1, size, step, 0)

    barrier = pltpu.get_barrier_semaphore()
    others(NT, ti, lambda t: pl.semaphore_signal(barrier, inc=1, device_id=(ci, t), device_id_type=MESH))
    others(NC, ci, lambda c: pl.semaphore_signal(barrier, inc=1, device_id=(c, ti), device_id_type=MESH))

    def push(src, dst, sems, device):
        pltpu.make_async_remote_copy(
            src_ref=src, dst_ref=dst, send_sem=sems[0], recv_sem=sems[1],
            device_id=device, device_id_type=MESH,
        ).start()

    def await_bytes(ref, sem):
        pltpu.make_async_copy(ref, ref, sem).wait()

    sub = lax.broadcasted_iota(I32, (NT, N), 0)
    lane = lax.broadcasted_iota(I32, (NT, N), 1)
    rank = ci // 2
    count = jnp.zeros((NT, N), I32)
    pick = jnp.zeros((NT, N), F32)
    for j in range(SLOTS):
        mine = sub == own[j]
        pick = jnp.where(mine & (lane == j) & (count == rank), 1.0, pick)
        count = jnp.where(mine, count + 1, count)
    pick = pick[:, :SLOTS].astype(BF16)
    loads[0].wait()
    first = lax.rem(ci, 2) == 0
    for i in range(8):
        row_a = kb[pl.ds(i // 2, SLOTS, stride=12), :]
        row_b = kb[pl.ds(4 + i, SLOTS, stride=12), :]
        row = jnp.where(first, row_a, row_b)
        high, rest = split(row)
        mid, low = split(row - high.astype(F32))
        del rest
        wsend[pl.ds(i, NT, stride=8), :] = dot(pick, high) + (dot(pick, mid) + dot(pick, low))

    pl.semaphore_wait(barrier, NT - 1 + NC - 1)

    others(NC, ci, lambda c: push(p_hbm, pbuf.at[ci], (ag_s, ag_r), (c, ti)))
    others(NT, ti, lambda t: push(
        wsend.at[pl.ds(pl.multiple_of(t * 8, 8), 8)], wbuf.at[ci, ti], (w1_s, w1_r), (ci, t)))
    own_w = pltpu.make_async_copy(wsend.at[pl.ds(pl.multiple_of(ti * 8, 8), 8)], wbuf.at[ci, ti], loc_sem.at[0])
    own_w.start()

    sub16 = lax.broadcasted_iota(I32, (16, 2 * N), 0)
    lane16 = lax.broadcasted_iota(I32, (16, 2 * N), 1)
    base16 = (sub16 & 1) * N + ((sub16 >> 1) & 3)

    def mark(h, carry):
        for half in range(2):
            start = jnp.where(sub16 < 8, offs[0, 0, h, 2 * half], offs[0, 0, h, 2 * half + 1])
            hit = jnp.where(lane16 == base16 + start, 1.0, 0.0).astype(BF16)
            onehot[pl.ds(pl.multiple_of(h * 32 + half * 16, 16), 16), :] = hit
        return carry

    lax.fori_loop(0, NT, mark, 0)
    loads[1].wait()

    def phases(g, carry):
        rows = pl.ds(pl.multiple_of(g * 256, 256), 256)
        hot = onehot[rows, :]
        for i in range(2):
            pt[i, rows, :] = dot(hot, tab[4 + i]).astype(BF16)
            pi[i, g] = lax.dot_general(
                tab[6 + i], hot, (((1,), (1,)), ((), ())), preferred_element_type=F32
            ).astype(BF16)
        return carry

    lax.fori_loop(0, 4, phases, 0)

    loads[2].wait()
    loads[3].wait()
    await_bytes(pbuf.at[pl.ds(0, NC - 1)], ag_r)
    left, right = (tab[0], tab[1]), (tab[2], tab[3])
    for pair in range(2):
        parts = []
        for xi in (2 * pair, 2 * pair + 1):
            p_re = pbuf[:, 0, xi].reshape(N, N)
            p_im = pbuf[:, 1, xi].reshape(N, N)
            s_re, s_im = smap[0, xi], smap[1, xi]
            parts.append(jnp.concatenate([s_re * p_re - s_im * p_im, s_re * p_im + s_im * p_re], axis=1))
        along_z = dot3(split(jnp.concatenate(parts, axis=0)), right)
        columns = [
            jnp.concatenate([along_z[i * N : (i + 1) * N, :N], along_z[i * N : (i + 1) * N, N:]], axis=0)
            for i in range(2)
        ]
        along_y = dot3(left, split(jnp.concatenate(columns, axis=1)))
        for i in range(2):
            for c in range(2):
                send1[pl.ds(c * 4 + 2 * pair + i, N, stride=8), :] = along_y[
                    c * N : (c + 1) * N, i * N : (i + 1) * N
                ]

    def rows_of(t):
        return pl.ds(pl.multiple_of(t * 32, 32), 32)

    others(NT, ti, lambda t: push(send1.at[rows_of(t)], recv1.at[ti], (a1_s, a1_r), (ci, t)))
    own_1 = pltpu.make_async_copy(send1.at[rows_of(ti)], recv1.at[ti], loc_sem.at[1])
    own_1.start()

    own_w.wait()
    await_bytes(wbuf.at[ci, pl.ds(0, NT - 1)], w1_r)
    others(NC, ci, lambda c: push(wbuf.at[ci], wbuf.at[ci], (w2_s, w2_r), (c, ti)))

    loads[5].wait()
    norm_part = jnp.sum(rv[...].reshape(16, 8, N) * rv[...].reshape(16, 8, N), axis=0)

    own_1.wait()
    await_bytes(recv1.at[pl.ds(0, NT - 1)], a1_r)
    for e in range(0, 4, 2):
        got = [recv1[:, (e + i) * 8 : (e + i + 1) * 8, :].reshape(2 * N, N) for i in range(2)]
        field = split(jnp.concatenate(got, axis=1))

        def cut(g, carry, e=e, field=field):
            rows = pl.ds(pl.multiple_of(g * 256, 256), 256)
            boxes[rows, e * N : (e + 2) * N] = dot3((pt[0, rows, :], pt[1, rows, :]), field)
            return carry

        lax.fori_loop(0, 4, cut, 0)

    await_bytes(wbuf.at[pl.ds(0, NC - 1)], w2_r)
    lane8 = lax.broadcasted_iota(I32, (8, N), 1)

    def regrid(h, total):
        for k in range(CAP):
            rows = pl.ds(pl.multiple_of(h * 32 + k * 8, 8), 8)
            w_x = wbuf[2 * k, h]
            w_yz = wbuf[2 * k + 1, h]
            start = offs[2, 0, h, k]
            here = [lane8 == start + f for f in range(4)]
            value = jnp.zeros((8, N), F32)
            for e in range(4):
                cells = boxes[rows, e * N : (e + 1) * N]
                inner = jnp.zeros((8, N), F32)
                for f in range(4):
                    cell = jnp.sum(jnp.where(here[f], cells, 0.0), axis=1, keepdims=True)
                    inner += cell * w_yz[4 + f : 5 + f, :]
                value += inner * w_yz[e : e + 1, :]
            value = value * w_x
            value = value + pltpu.roll(value, 4, 0)
            value = value + pltpu.roll(value, 2, 0)
            total = total + value * value
            value = value * w_x
            for e in range(4):
                weighted = value * w_yz[e : e + 1, :]
                cells = jnp.zeros((8, N), F32)
                for f in range(4):
                    cell = jnp.sum(weighted * w_yz[4 + f : 5 + f, :], axis=1, keepdims=True)
                    cells = jnp.where(here[f], cell, cells)
                placed[rows, e * N : (e + 1) * N] = cells
        return total

    product_part = lax.fori_loop(0, NT, regrid, jnp.zeros((8, N), F32)) * 0.25

    for e in range(0, 4, 2):
        gacc[...] = jnp.zeros_like(gacc)

        def place(g, carry, e=e):
            rows = pl.ds(pl.multiple_of(g * 256, 256), 256)
            gacc[...] += dot3((pi[0, g], pi[1, g]), split(placed[rows, e * N : (e + 2) * N]))
            return carry

        lax.fori_loop(0, 4, place, 0)
        for i in range(2):
            send2[:, (e + i) * 8 : (e + i + 1) * 8, :] = gacc[:, i * N : (i + 1) * N].reshape(NT, 8, N)

    others(NT, ti, lambda t: push(send2.at[t], recv2.at[rows_of(ti)], (a2_s, a2_r), (ci, t)))
    own_2 = pltpu.make_async_copy(send2.at[ti], recv2.at[rows_of(ti)], loc_sem.at[2])
    own_2.start()

    row8 = lax.broadcasted_iota(I32, (8, N), 0)
    norm_row = jnp.sum(norm_part, axis=0, keepdims=True)
    product_row = jnp.sum(product_part, axis=0, keepdims=True)
    ar1[0] = jnp.where(row8 == 0, norm_row, jnp.where(row8 == 1, product_row, 0.0))
    others(NC, ci, lambda c: push(ar1.at[0], ar1c.at[ci], (r1c_s, r1c_r), (c, ti)))
    ar1c[ci] = ar1[0]
    await_bytes(ar1c.at[pl.ds(0, NC - 1)], r1c_r)
    ar1[1] = jnp.sum(ar1c[...], axis=0)
    others(NT, ti, lambda t: push(ar1.at[1], ar1t.at[ti], (r1t_s, r1t_r), (ci, t)))
    ar1t[ti] = ar1[1]

    own_2.wait()
    await_bytes(recv1.at[pl.ds(0, NT - 1)], a2_r)
    for pair in range(2):
        columns = [
            jnp.concatenate([recv2[pl.ds(c * 4 + 2 * pair + i, N, stride=8), :] for c in range(2)], axis=0)
            for i in range(2)
        ]
        along_y = dot3(right, split(jnp.concatenate(columns, axis=1)))
        parts = [
            jnp.concatenate([along_y[:N, i * N : (i + 1) * N], along_y[N:, i * N : (i + 1) * N]], axis=1)
            for i in range(2)
        ]
        along_z = dot3(split(jnp.concatenate(parts, axis=0)), left)
        for i in range(2):
            xi = 2 * pair + i
            m_re = along_z[i * N : (i + 1) * N, :N]
            m_im = along_z[i * N : (i + 1) * N, N:]
            s_re, s_im = smap[0, xi], smap[1, xi]
            rs_send[:, 0, xi] = (s_re * m_re + s_im * m_im).reshape(NC, 16, N)
            rs_send[:, 1, xi] = (s_re * m_im - s_im * m_re).reshape(NC, 16, N)

    others(NC, ci, lambda c: push(rs_send.at[c], rs_recv.at[ci], (rs_s, rs_r), (c, ti)))
    own_3 = pltpu.make_async_copy(rs_send.at[ci], rs_recv.at[ci], loc_sem.at[3])
    own_3.start()

    loads[4].wait()
    await_bytes(ar1t.at[pl.ds(0, NT - 1)], r1t_r)
    sums = jnp.sum(jnp.sum(ar1t[...], axis=0), axis=1, keepdims=True)
    norm_now, product = sums[0:1], sums[1:2]
    alpha = norm_now / product
    nx[...] = (xv[...].reshape(N, N) + alpha * pbuf[ci].reshape(N, N)).reshape(nx.shape)
    out_x = pltpu.make_async_copy(nx, ox_hbm, out_sem.at[0])
    out_x.start()

    own_3.wait()
    await_bytes(rs_recv.at[pl.ds(0, NC - 1)], rs_r)
    normal = jnp.sum(rs_recv[...], axis=0).reshape(N, N)
    next_r = rv[...].reshape(N, N) - alpha * normal
    nr[...] = next_r.reshape(nr.shape)
    out_r = pltpu.make_async_copy(nr, or_hbm, out_sem.at[1])
    out_r.start()

    ar2[0] = jnp.sum((next_r * next_r).reshape(16, 8, N), axis=0)
    others(NC, ci, lambda c: push(ar2.at[0], ar2c.at[ci], (r2c_s, r2c_r), (c, ti)))
    ar2c[ci] = ar2[0]
    await_bytes(ar2c.at[pl.ds(0, NC - 1)], r2c_r)
    ar2[1] = jnp.sum(ar2c[...], axis=0)
    others(NT, ti, lambda t: push(ar2.at[1], ar2t.at[ti], (r2t_s, r2t_r), (ci, t)))
    ar2t[ti] = ar2[1]
    await_bytes(ar2t.at[pl.ds(0, NT - 1)], r2t_r)
    norm_next = jnp.sum(jnp.sum(jnp.sum(ar2t[...], axis=0), axis=0, keepdims=True), axis=1, keepdims=True)
    beta = norm_next / norm_now
    npv[...] = (nr[...].reshape(N, N) + beta * pbuf[ci].reshape(N, N)).reshape(npv.shape)
    out_p = pltpu.make_async_copy(npv, op_hbm, out_sem.at[2])
    out_p.start()

    await_bytes(pbuf.at[pl.ds(0, NC - 1)], ag_s)
    await_bytes(wbuf.at[0, pl.ds(0, NT - 1)], w1_s)
    await_bytes(wbuf.at[pl.ds(0, NC - 1)], w2_s)
    await_bytes(recv1.at[pl.ds(0, NT - 1)], a1_s)
    await_bytes(recv1.at[pl.ds(0, NT - 1)], a2_s)
    await_bytes(rs_recv.at[pl.ds(0, NC - 1)], rs_s)
    await_bytes(ar1c.at[pl.ds(0, NC - 1)], r1c_s)
    await_bytes(ar1t.at[pl.ds(0, NT - 1)], r1t_s)
    await_bytes(ar2c.at[pl.ds(0, NC - 1)], r2c_s)
    await_bytes(ar2t.at[pl.ds(0, NT - 1)], r2t_s)
    out_x.wait()
    out_r.wait()
    out_p.wait()


def shards(image_p, image_x, image_r, sensitivity, kb_weights, block_owner, owner_list):
    shard = image_p.shape
    vmem = pltpu.VMEM
    dma = pltpu.SemaphoreType.DMA
    scratch = [
        vmem((8, 2 * N, 2 * N), BF16),
        vmem((2, 4, N, N), F32),
        vmem((SLOTS * 12, N), F32),
        vmem(shard, F32),
        vmem(shard, F32),
        vmem((NC,) + shard, F32),
        vmem((NT * 8, N), F32),
        vmem((NC, NT, 8, N), F32),
        vmem((8 * N, 2 * N), BF16),
        vmem((2, 8 * N, 2 * N), BF16),
        vmem((2, 4, 2 * N, 2 * N), BF16),
        vmem((8 * N, N), F32),
        vmem((NT, 32, N), F32),
        vmem((8 * N, 4 * N), F32),
        vmem((8 * N, 4 * N), F32),
        vmem((2 * N, 2 * N), F32),
        vmem((NT, 32, N), F32),
        vmem((8 * N, N), F32),
        vmem((NC,) + shard, F32),
        vmem((NC,) + shard, F32),
        vmem(shard, F32),
        vmem(shard, F32),
        vmem(shard, F32),
        vmem((2, 8, N), F32),
        vmem((NC, 8, N), F32),
        vmem((NT, 8, N), F32),
        vmem((2, 8, N), F32),
        vmem((NC, 8, N), F32),
        vmem((NT, 8, N), F32),
        dma((6,)),
        dma((4,)),
    ]
    scratch += [dma(())] * 20 + [dma((3,))]
    out = jax.ShapeDtypeStruct(shard, F32)
    return pl.pallas_call(
        kernel,
        out_shape=(out, out, out),
        in_specs=[ANY] * 5 + [SMEM] * 2 + [ANY],
        out_specs=(ANY, ANY, ANY),
        scratch_shapes=scratch,
        compiler_params=pltpu.CompilerParams(
            collective_id=0, has_side_effects=True, vmem_limit_bytes=48 * 2**20
        ),
    )(
        image_p, image_x, image_r, sensitivity, kb_weights.reshape(SLOTS * 12, N),
        block_owner, owner_list, jnp.asarray(tables()),
    )


def solution(mesh):
    image = P(None, "tile", "coil", None)
    return jax.shard_map(
        shards,
        mesh=mesh,
        in_specs=(
            image, image, image,
            P("coil", None, "tile", None, None),
            P("tile", None, None, None),
            P("tile"),
            P(None, "tile", None, None),
        ),
        out_specs=(image, image, image),
        check_vma=False,
    )
```

profile of v0, /device:TPU:1, one launch (start us, length us, event | category | flops | bytes accessed | tf_op | source)
XLA Modules:
  0.0 93.2 jit_solution(16168574976782609459)
XLA Ops:
  0.6 0.0 copy-start.6
  0.6 0.8 copy.11.offs
  1.4 0.0 copy-done.6
  1.4 0.0 copy-start
  1.4 1.2 %copy-done = bf16[8,256,256]{2,1,0:T(8,128)(2,1)S(1)} copy-done((bf16[8,256,256]{2,1,0:T(8,128)(2,1)S(1)}, bf16[8,256,256]{2,1,0:T(8,128)(2,1)}, u32[]{:S(2)}) %copy-start) | copy-done | bytes 1048600
  2.7 0.0 copy-start.1
  2.7 1.0 %copy-done.1 = f32[1,2,4,128,128]{4,3,2,1,0:T(8,128)S(1)} copy-done((f32[1,2,4,128,128]{4,3,2,1,0:T(8,128)S(1)}, f32[1,2,4,128,128]{4,3,2,1,0:T(8,128)}, u32[]{:S(2)}) %copy-start.1) | copy-done | bytes 524312
  3.7 0.0 copy-start.2
  3.7 0.9 copy-done.2
  4.6 0.0 copy-start.3
  4.6 0.8 copy-done.3
  5.5 0.0 copy-start.4
  5.5 0.8 copy-done.4
  6.3 0.0 copy-start.5
  6.3 0.8 copy-done.5
  7.1 84.2 %shard_map.103 = (f32[2,4,16,128]{3,2,1,0:T(8,128)S(1)}, f32[2,4,16,128]{3,2,1,0:T(8,128)S(1)}, f32[2,4,16,128]{3,2,1,0:T(8,128)S(1)}) custom-call(f32[2,4,16,128]{3,2,1,0:T(8,128)S(1)} %copy-done.3, f32[2,4,16,128]{3,2,1,0:T(8,128)S(1)} %copy-done.4, f32[2,4,16,128]{3,2,1,0:T(8,128)S(1)} %copy-done.5, f32[1,2,4,128,128]{4,3,2,1,0:T(8,128)S(1)} %copy-done.1, ...), custom_call_target="tpu_custom_call" | custom-call | tf_op jit(solution)/shard_map/pallas_call | solution.py:375
  91.3 0.6 copy.15
  92.0 0.6 copy.16
  92.6 0.6 copy.17
Async XLA Ops:
  0.6 0.8 copy-start.6
  1.4 1.2 %copy-start = (bf16[8,256,256]{2,1,0:T(8,128)(2,1)S(1)}, bf16[8,256,256]{2,1,0:T(8,128)(2,1)}, u32[]{:S(2)}) copy-start(bf16[8,256,256]{2,1,0:T(8,128)(2,1)} %constant.2.clone.tab_hbm) | copy-start | bytes 3145732
  2.7 1.0 %copy-start.1 = (f32[1,2,4,128,128]{4,3,2,1,0:T(8,128)S(1)}, f32[1,2,4,128,128]{4,3,2,1,0:T(8,128)}, u32[]{:S(2)}) copy-start(f32[1,2,4,128,128]{4,3,2,1,0:T(8,128)} %s_hbm.1) | copy-start | bytes 1572868
  3.7 0.9 copy-start.2
  4.6 0.8 copy-start.3
  5.5 0.8 copy-start.4
  6.3 0.8 copy-start.5
where the time goes:
time: 93.6 us; the launch traced here: 93.2 us
  Pallas kernels  84.2 us (90%)
  local copies, waits for them, and re-layouts  8.39 us (9%)
    pallas_call x1, Pallas kernels, shards(): pl.pallas_call(kernel, out_shape=(out, out, out), in_specs=[ANY] * 5 + [S...  84.2 us
    unnamed x18, local copies, waits for them, and re-layouts  8.39 us

commit v1 on v0

v1 whole, which is shorter than its diff:
```python
import functools
import math

import jax
import jax.numpy as jnp
import ml_dtypes
import numpy as np
from jax import lax
from jax.experimental import pallas as pl
from jax.experimental.pallas import tpu as pltpu
from jax.sharding import PartitionSpec as P

N = 128
NC = 8
NT = 32
CAP = 4
SLOTS = 32
F32, BF16, I32 = jnp.float32, jnp.bfloat16, jnp.int32
MESH = pl.DeviceIdType.MESH
HBM = pl.BlockSpec(memory_space=pltpu.HBM)
SMEM = pl.BlockSpec(memory_space=pltpu.SMEM)


def tables():
    cells = np.arange(N)
    angle = 2.0 * math.pi / N * ((cells[:, None] * cells[None, :]) % N)
    cos, sin = np.cos(angle) / math.sqrt(N), np.sin(angle) / math.sqrt(N)
    left = np.block([[cos, sin], [-sin, cos]])
    order = [c * N + 4 * t + i for t in range(NT) for c in range(2) for i in range(4)]
    out = []
    for table in (left, left.T, left[:, order], left[:, order].T):
        table = table.astype(np.float32)
        high = table.astype(ml_dtypes.bfloat16)
        low = (table - high.astype(np.float32)).astype(ml_dtypes.bfloat16)
        out += [high, low]
    return np.stack(out)


def split(x):
    high = x.astype(BF16)
    return high, (x - high.astype(F32)).astype(BF16)


def dot(a, b):
    return jnp.dot(a, b, preferred_element_type=F32)


def dot_t(a, b):
    return lax.dot_general(a, b, (((1,), (1,)), ((), ())), preferred_element_type=F32)


def dot3(a, b):
    return dot(a[0], b[0]) + (dot(a[0], b[1]) + dot(a[1], b[0]))


def kernel(
    p_hbm, r_hbm, s_hbm, kb_hbm, own, offs, tab_hbm,
    normal_hbm, alpha_hbm, beta_hbm,
    tab, smap, kb, rv, pbuf, wsend, wbuf, onehot, pt, pi,
    send1, recv1, boxes, placed, send2, recv2, rs_send, rs_near, rs_sum, rs_recv,
    nv, alphas, betas, ar1, ar1c, ar1z, ar1y, ar2, ar2c, ar2z, ar2y,
    load_sem, loc_sem, ag_s, ag_r, agf_s, agf_r, w1_s, w1_r, a1_s, a1_r, a2_s, a2_r, w2f_s, w2f_r, w2_s, w2_r,
    rn_s, rn_r, rs_s, rs_r, r1_s, r1_r, r2_s, r2_r, out_sem,
):
    ci, ti = lax.axis_index("coil"), lax.axis_index("tile")
    core, cx = lax.rem(ci, 2), ci // 2
    near = ci + 1 - 2 * core
    z, y = ti // 4, lax.rem(ti, 4)

    loads = [
        pltpu.make_async_copy(src, dst, load_sem.at[i])
        for i, (src, dst) in enumerate(
            [
                (kb_hbm, kb),
                (tab_hbm, tab),
                (s_hbm.at[0], smap),
                (p_hbm, pbuf.at[ci]),
                (r_hbm, rv),
            ]
        )
    ]

    def partner(me, size, i):
        return lax.rem(me + size // 2 + (i + 1) // 2 * (1 - 2 * lax.rem(i, 2)), size)

    def tiles(body, first=0, last=NT - 1):
        def step(i, carry):
            body(partner(z, 8, lax.rem(i, 8)) * 4 + partner(y, 4, i // 8))
            return carry

        lax.fori_loop(first, last, step, 0)

    def ring(me, size, body):
        def step(i, carry):
            body(partner(me, size, i))
            return carry

        lax.fori_loop(0, size - 1, step, 0)

    barrier = pltpu.get_barrier_semaphore()
    tiles(lambda t: pl.semaphore_signal(barrier, inc=1, device_id=(ci, t), device_id_type=MESH))
    ring(ci, NC, lambda c: pl.semaphore_signal(barrier, inc=1, device_id=(c, ti), device_id_type=MESH))
    for load in loads:
        load.start()

    def push(src, dst, sems, device):
        pltpu.make_async_remote_copy(
            src_ref=src, dst_ref=dst, send_sem=sems[0], recv_sem=sems[1],
            device_id=device, device_id_type=MESH,
        ).start()

    def await_bytes(ref, sem):
        pltpu.make_async_copy(ref, ref, sem).wait()

    class Sum:
        def __init__(self, part, held, slots, sems):
            self.part, self.held, self.slots, self.sems, self.stage = part, held, slots, sems, 0

        def send(self):
            stage = self.stage
            slot, sems = self.slots[stage], (self.sems[0].at[stage], self.sems[1].at[stage])
            self.held[stage] = self.part
            src = self.held.at[stage]
            me = (ci, z, y)[stage]
            device = (lambda i: (i, ti), lambda i: (ci, i * 4 + y), lambda i: (ci, z * 4 + i))[stage]
            ring(me, slot.shape[0], lambda i: push(src, slot.at[me], sems, device(i)))
            slot[me] = self.part

        def take(self):
            slot = self.slots[self.stage]
            await_bytes(slot.at[pl.ds(0, slot.shape[0] - 1)], self.sems[1].at[self.stage])
            self.part = jnp.sum(slot[...], axis=0)
            self.stage += 1
            return self.part

        def sent(self):
            for stage, slot in enumerate(self.slots):
                await_bytes(slot.at[pl.ds(0, slot.shape[0] - 1)], self.sems[0].at[stage])

    sub = lax.broadcasted_iota(I32, (NT, N), 0)
    lane = lax.broadcasted_iota(I32, (NT, N), 1)
    count = jnp.zeros((NT, N), I32)
    pick = jnp.zeros((NT, N), F32)
    for j in range(SLOTS):
        mine = sub == own[j]
        pick = jnp.where(mine & (lane == j) & (count == cx), 1.0, pick)
        count = jnp.where(mine, count + 1, count)
    pick = pick[:, :SLOTS].astype(BF16)
    loads[0].wait()
    for i in range(8):
        row_a = kb[pl.ds(i // 2, SLOTS, stride=12), :]
        row_b = kb[pl.ds(4 + i, SLOTS, stride=12), :]
        row = jnp.where(core == 0, row_a, row_b)
        high = row.astype(BF16)
        mid, low = split(row - high.astype(F32))
        wsend[pl.ds(i, NT, stride=8), :] = dot(pick, high) + (dot(pick, mid) + dot(pick, low))

    pl.semaphore_wait(barrier, NT - 1 + NC - 1)

    def chip(k):
        return lax.rem(ci + 2 * k, NC)

    loads[3].wait()
    mine = pbuf.at[ci]
    for k in (2, 1, 3):
        push(mine, mine, (ag_s.at[k - 1], ag_r.at[k - 1]), (chip(k), ti))
    push(mine, mine, (agf_s, agf_r), (near, ti))

    def send_weights(first, last):
        tiles(lambda t: push(
            wsend.at[pl.ds(pl.multiple_of(t * 8, 8), 8)], wbuf.at[ci, ti], (w1_s, w1_r), (ci, t)), first, last)

    own_w = pltpu.make_async_copy(wsend.at[pl.ds(pl.multiple_of(ti * 8, 8), 8)], wbuf.at[ci, ti], loc_sem.at[0])
    own_w.start()
    send_weights(0, 16)
    for k in (1, 3, 2):
        came = pbuf.at[chip(4 - k)]
        await_bytes(came, ag_r.at[k - 1])
        push(came, came, (agf_s, agf_r), (near, ti))
        if k == 3:
            send_weights(16, 24)
    send_weights(24, NT - 1)

    sub16 = lax.broadcasted_iota(I32, (16, 2 * N), 0)
    lane16 = lax.broadcasted_iota(I32, (16, 2 * N), 1)
    base16 = (sub16 & 1) * N + ((sub16 >> 1) & 3)

    def mark(h, carry):
        for half in range(2):
            start = jnp.where(sub16 < 8, offs[0, 0, 2 * half, h], offs[0, 0, 2 * half + 1, h])
            hit = jnp.where(lane16 == base16 + start, 1.0, 0.0).astype(BF16)
            onehot[pl.ds(pl.multiple_of(h * 32 + half * 16, 16), 16), :] = hit
        return carry

    lax.fori_loop(0, NT, mark, 0)
    loads[1].wait()

    def phases(g, carry):
        rows = pl.ds(pl.multiple_of(g * 256, 256), 256)
        hot = onehot[rows, :]
        for i in range(2):
            pt[i, rows, :] = dot(hot, tab[4 + i]).astype(BF16)
        return carry

    lax.fori_loop(0, 4, phases, 0)
    for i in range(2):
        for g in range(4):
            columns = slice(g * 256, (g + 1) * 256)
            pi[i, :, columns] = dot_t(tab[6 + i], onehot[columns, :]).astype(BF16)

    loads[2].wait()
    await_bytes(pbuf.at[pl.ds(0, 4)], agf_r)
    left, right = (tab[0], tab[1]), (tab[2], tab[3])
    for pair in range(2):
        parts = []
        for xi in (2 * pair, 2 * pair + 1):
            p_re = pbuf[:, 0, xi].reshape(N, N)
            p_im = pbuf[:, 1, xi].reshape(N, N)
            s_re, s_im = smap[0, xi], smap[1, xi]
            parts.append(jnp.concatenate([s_re * p_re - s_im * p_im, s_re * p_im + s_im * p_re], axis=1))
        along_z = dot3(split(jnp.concatenate(parts, axis=0)), right)
        columns = [
            jnp.concatenate([along_z[i * N : (i + 1) * N, :N], along_z[i * N : (i + 1) * N, N:]], axis=0)
            for i in range(2)
        ]
        along_y = dot3(left, split(jnp.concatenate(columns, axis=1)))
        for i in range(2):
            for c in range(2):
                send1[pl.ds(c * 4 + 2 * pair + i, N, stride=8), :] = along_y[
                    c * N : (c + 1) * N, i * N : (i + 1) * N
                ]

    def rows_of(t):
        return pl.ds(pl.multiple_of(t * 32, 32), 32)

    own_w.wait()
    await_bytes(wbuf.at[ci, pl.ds(0, NT - 1)], w1_r)
    for k in (2, 1, 3):
        push(wbuf.at[ci], wbuf.at[ci], (w2_s.at[k - 1], w2_r.at[k - 1]), (chip(k), ti))
    tiles(lambda t: push(send1.at[rows_of(t)], recv1.at[ti], (a1_s, a1_r), (ci, t)))
    own_1 = pltpu.make_async_copy(send1.at[rows_of(ti)], recv1.at[ti], loc_sem.at[1])
    own_1.start()

    push(wbuf.at[ci], wbuf.at[ci], (w2f_s, w2f_r), (near, ti))
    for k in (1, 3, 2):
        came = wbuf.at[chip(4 - k)]
        await_bytes(came, w2_r.at[k - 1])
        push(came, came, (w2f_s, w2f_r), (near, ti))

    loads[4].wait()
    norm_part = jnp.sum(rv[...].reshape(16, 8, N) * rv[...].reshape(16, 8, N), axis=0)

    own_1.wait()
    await_bytes(recv1.at[pl.ds(0, NT - 1)], a1_r)
    for e in range(0, 4, 2):
        got = [recv1[:, (e + i) * 8 : (e + i + 1) * 8, :].reshape(2 * N, N) for i in range(2)]
        field = split(jnp.concatenate(got, axis=1))

        def cut(g, carry, e=e, field=field):
            rows = pl.ds(pl.multiple_of(g * 256, 256), 256)
            boxes[rows, e * N : (e + 2) * N] = dot3((pt[0, rows, :], pt[1, rows, :]), field)
            return carry

        lax.fori_loop(0, 4, cut, 0)

    await_bytes(wbuf.at[pl.ds(0, 4)], w2f_r)
    lane8 = lax.broadcasted_iota(I32, (8, N), 1)
    low8 = lax.broadcasted_iota(I32, (8, N), 0) < 4

    def regrid(g, total):
        spread, pairs, w_xs, starts = [], [], [], []
        for b in range(8):
            h, k = 2 * g + b // 4, b % 4
            w_xs.append(wbuf[2 * k, h])
            w_yz = wbuf[2 * k + 1, h]
            w_z = jnp.where(low8, pltpu.roll(w_yz, 4, 0), w_yz)
            for e in (0, 2):
                pairs.append(jnp.where(low8, w_yz[e : e + 1, :], w_yz[e + 1 : e + 2, :]) * w_z)
            start = offs[2, 0, k, h]
            starts.append(start)
            rows = pl.ds(pl.multiple_of(g * 64 + b * 8, 8), 8)
            moved = jnp.zeros((8, N), F32)
            for e in range(4):
                at = b * 16 + e * 4
                cells = pltpu.roll(boxes[rows, e * N : (e + 1) * N], lax.rem(at + 2 * N - start, N), 1)
                moved = jnp.where((lane8 >= at) & (lane8 < at + 4), cells, moved)
            spread.append(moved)
        pairs = split(jnp.concatenate(pairs, axis=0))
        values = dot3(split(jnp.concatenate(spread, axis=0)), pairs)
        back = []
        for b in range(8):
            value = values[b * 8 : (b + 1) * 8] * w_xs[b]
            value = value + pltpu.roll(value, 4, 0)
            value = value + pltpu.roll(value, 2, 0)
            total = total + value * value
            back.append(value * w_xs[b])
        back = split(jnp.concatenate(back, axis=0))
        cells = dot_t(back[0], pairs[0]) + (dot_t(back[0], pairs[1]) + dot_t(back[1], pairs[0]))
        rows = pl.ds(pl.multiple_of(g * 64, 64), 64)
        for e in range(4):
            parts = []
            for b in range(8):
                at = b * 16 + e * 4
                moved = pltpu.roll(cells[b * 8 : (b + 1) * 8], lax.rem(starts[b] + 2 * N - at, N), 1)
                here = (lane8 >= starts[b]) & (lane8 < starts[b] + 4)
                parts.append(jnp.where(here, moved, 0.0))
            high, low = split(jnp.concatenate(parts, axis=0))
            placed[0, rows, e * N : (e + 1) * N] = high
            placed[1, rows, e * N : (e + 1) * N] = low
        return total

    product_part = lax.fori_loop(0, NT // 2, regrid, jnp.zeros((8, N), F32), unroll=4) * 0.25

    row8 = lax.broadcasted_iota(I32, (8, N), 0)
    norm_row = jnp.sum(norm_part, axis=0, keepdims=True)
    product_row = jnp.sum(product_part, axis=0, keepdims=True)
    both = jnp.where(row8 == 0, norm_row, jnp.where(row8 == 1, product_row, 0.0))
    first_sum = Sum(both, ar1, (ar1c, ar1z, ar1y), (r1_s, r1_r))
    first_sum.send()

    for e in range(0, 4, 2):
        columns = slice(e * N, (e + 2) * N)
        back = dot3((pi[0], pi[1]), (placed[0, :, columns], placed[1, :, columns]))
        for i in range(2):
            send2[:, (e + i) * 8 : (e + i + 1) * 8, :] = back[:, i * N : (i + 1) * N].reshape(NT, 8, N)
    first_sum.take()
    first_sum.send()

    tiles(lambda t: push(send2.at[t], recv2.at[rows_of(ti)], (a2_s, a2_r), (ci, t)))
    own_2 = pltpu.make_async_copy(send2.at[ti], recv2.at[rows_of(ti)], loc_sem.at[2])
    own_2.start()

    first_sum.take()
    first_sum.send()

    own_2.wait()
    await_bytes(recv1.at[pl.ds(0, NT - 1)], a2_r)
    for pair in range(2):
        columns = [
            jnp.concatenate([recv2[pl.ds(c * 4 + 2 * pair + i, N, stride=8), :] for c in range(2)], axis=0)
            for i in range(2)
        ]
        along_y = dot3(right, split(jnp.concatenate(columns, axis=1)))
        parts = [
            jnp.concatenate([along_y[:N, i * N : (i + 1) * N], along_y[N:, i * N : (i + 1) * N]], axis=1)
            for i in range(2)
        ]
        along_z = dot3(split(jnp.concatenate(parts, axis=0)), left)
        for i in range(2):
            m_re = along_z[i * N : (i + 1) * N, :N]
            m_im = along_z[i * N : (i + 1) * N, N:]
            s_re, s_im = smap[0, 2 * pair + i], smap[1, 2 * pair + i]
            for c, back in enumerate((s_re * m_re + s_im * m_im, s_re * m_im - s_im * m_re)):
                back = back.reshape(4, 2, 16, N)
                for half in range(2):
                    rs_send[half, pair, :, c, i] = back[:, half]
        push(rs_send.at[1 - core, pair], rs_near.at[pair], (rn_s.at[pair], rn_r.at[pair]), (near, ti))

    for pair in range(2):
        await_bytes(rs_near.at[pair], rn_r.at[pair])
        rs_sum[pair] = rs_send[core, pair] + rs_near[pair]
        for k in (2, 1, 3):
            to = lax.rem(cx + k, 4)
            push(rs_sum.at[pair, to], rs_recv.at[pair, cx], (rs_s.at[pair], rs_r.at[pair]), (chip(k), ti))
        rs_recv[pair, cx] = rs_sum[pair, cx]
    sums = jnp.sum(first_sum.take(), axis=1, keepdims=True)
    norm_now, product = sums[0:1], sums[1:2]
    alpha = norm_now / product
    norm_next = jnp.zeros((8, N), F32)
    for pair in range(2):
        await_bytes(rs_recv.at[pair, pl.ds(0, 3)], rs_r.at[pair])
        normal = jnp.sum(rs_recv[pair], axis=0)
        nv[:, 2 * pair : 2 * pair + 2] = normal
        next_r = rv[:, 2 * pair : 2 * pair + 2].reshape(64, N) - alpha * normal.reshape(64, N)
        norm_next += jnp.sum((next_r * next_r).reshape(8, 8, N), axis=0)
    out_n = pltpu.make_async_copy(nv, normal_hbm, out_sem.at[0])
    out_n.start()

    alphas[...] = jnp.broadcast_to(alpha, (1, N)).reshape(alphas.shape)
    out_a = pltpu.make_async_copy(alphas, alpha_hbm, out_sem.at[1])
    out_a.start()

    last_sum = Sum(norm_next, ar2, (ar2c, ar2z, ar2y), (r2_s, r2_r))
    for _ in range(3):
        last_sum.send()
        sums = last_sum.take()
    sums = jnp.sum(jnp.sum(sums, axis=0, keepdims=True), axis=1, keepdims=True)
    betas[...] = jnp.broadcast_to(sums / norm_now, (1, N)).reshape(betas.shape)
    out_b = pltpu.make_async_copy(betas, beta_hbm, out_sem.at[2])
    out_b.start()

    for k in range(3):
        await_bytes(pbuf.at[0], ag_s.at[k])
    await_bytes(pbuf.at[pl.ds(0, 4)], agf_s)
    await_bytes(wbuf.at[0, pl.ds(0, NT - 1)], w1_s)
    for k in range(3):
        await_bytes(wbuf.at[0], w2_s.at[k])
    await_bytes(wbuf.at[pl.ds(0, 4)], w2f_s)
    await_bytes(recv1.at[pl.ds(0, NT - 1)], a1_s)
    await_bytes(recv1.at[pl.ds(0, NT - 1)], a2_s)
    for pair in range(2):
        await_bytes(rs_near.at[pair], rn_s.at[pair])
        await_bytes(rs_recv.at[pair, pl.ds(0, 3)], rs_s.at[pair])
    first_sum.sent()
    last_sum.sent()
    out_n.wait()
    out_a.wait()
    out_b.wait()


def shards(image_p, image_x, image_r, sensitivity, kb_weights, block_owner, owner_list):
    shard = image_p.shape
    vmem = pltpu.VMEM
    dma = pltpu.SemaphoreType.DMA
    scratch = [
        vmem((8, 2 * N, 2 * N), BF16),
        vmem((2, 4, N, N), F32),
        vmem((SLOTS * 12, N), F32),
        vmem(shard, F32),
        vmem((NC,) + shard, F32),
        vmem((NT * 8, N), F32),
        vmem((NC, NT, 8, N), F32),
        vmem((8 * N, 2 * N), BF16),
        vmem((2, 8 * N, 2 * N), BF16),
        vmem((2, 2 * N, 8 * N), BF16),
        vmem((8 * N, N), F32),
        vmem((NT, 32, N), F32),
        vmem((8 * N, 4 * N), F32),
        vmem((2, 8 * N, 4 * N), BF16),
        vmem((NT, 32, N), F32),
        vmem((8 * N, N), F32),
        vmem((2, 2, 4, 2, 2, 16, N), F32),
        vmem((2, 4, 2, 2, 16, N), F32),
        vmem((2, 4, 2, 2, 16, N), F32),
        vmem((2, 4, 2, 2, 16, N), F32),
        vmem(shard, F32),
        vmem((1, 1, 1, N), F32),
        vmem((1, 1, 1, N), F32),
    ]
    for _ in range(2):
        scratch += [vmem((3, 8, N), F32)] + [vmem((n, 8, N), F32) for n in (NC, 8, 4)]
    scratch += [dma((n,)) for n in (5, 3, 3, 3)] + [dma(())] * 10
    scratch += [dma((3,))] * 2 + [dma((2,))] * 4 + [dma((3,))] * 5
    step = jax.ShapeDtypeStruct((1, 1, 1, N), F32)
    normal, alpha, beta = pl.pallas_call(
        kernel,
        out_shape=(jax.ShapeDtypeStruct(shard, F32), step, step),
        in_specs=[HBM] * 4 + [SMEM] * 2 + [HBM],
        out_specs=(HBM, HBM, HBM),
        scratch_shapes=scratch,
        compiler_params=pltpu.CompilerParams(
            collective_id=0, has_side_effects=True, vmem_limit_bytes=60 * 2**20
        ),
    )(
        image_p, image_r, sensitivity, kb_weights.reshape(SLOTS * 12, N),
        block_owner, owner_list.transpose(0, 1, 3, 2), jnp.asarray(tables()),
    )
    next_x = image_x + alpha * image_p
    next_r = image_r - alpha * normal
    next_p = next_r + beta * image_p
    return next_x, next_r, next_p


def solution(mesh):
    image = P(None, "tile", "coil", None)
    return jax.shard_map(
        shards,
        mesh=mesh,
        in_specs=(
            image, image, image,
            P("coil", None, "tile", None, None),
            P("tile", None, None, None),
            P("tile"),
            P(None, "tile", None, None),
        ),
        out_specs=(image, image, image),
        check_vma=False,
    )
```

time: 93.6 us -> 80.4 us (0.86)
  local copies, waits for them, and re-layouts: 8.39 us -> 0.64 us
  Pallas kernels: 84.2 us -> 77.3 us
  other arithmetic: 0 us -> 1.53 us
    unnamed x18 -> x10, local copies, waits for them, and re-layouts: 8.39 us -> 0.64 us
    pallas_call x1, Pallas kernels: 84.2 us -> 77.3 us  [shards(): pl.pallas_call(kernel, out_shape=(jax.ShapeDtypeStruct(shard, F32), step,...]
    add x0 -> x1, other arithmetic: none -> 1.53 us  [shards(): next_p = next_r + beta * image_p]
where the time goes in v1:
time: 80.4 us; the launch traced here: 80.2 us
  Pallas kernels  77.3 us (96%)
  other arithmetic  1.53 us (2%)
    pallas_call x1, Pallas kernels, shards(): pl.pallas_call(kernel, out_shape=(jax.ShapeDtypeStruct(shard, F32), step,...  77.3 us

profile of v1, /device:TPU:1, one launch (start us, length us, event | category | flops | bytes accessed | tf_op | source)
XLA Modules:
  0.0 80.2 jit_solution(492929867077699308)
XLA Ops:
  0.6 0.0 copy-start
  0.6 0.0 copy-start.1
  0.7 0.0 copy-start.2
  0.7 77.3 %shard_map.103 = (f32[2,4,16,128]{3,2,1,0:T(8,128)}, f32[1,1,1,128]{3,2,1,0:T(1,128)}, f32[1,1,1,128]{3,2,1,0:T(1,128)}) custom-call(f32[2,4,16,128]{3,2,1,0:T(8,128)} %p_hbm.1, f32[2,4,16,128]{3,2,1,0:T(8,128)} %r_hbm.1, f32[1,2,4,128,128]{4,3,2,1,0:T(8,128)} %s_hbm.1, f32[384,128]{1,0:T(8,128)} %bitcast.4, s32[32]{0:T(128)} %own.1, ...), custom_call_target="tpu_custom_call" | custom-call | tf_op jit(solution)/shard_map/pallas_call | solution.py:445
  78.0 0.0 copy-start.3
  78.0 0.0 copy-start.4
  78.0 0.0 copy-done
  78.0 0.0 copy-done.1
  78.1 0.0 copy-done.2
  78.1 0.6 copy-done.3
  78.6 0.1 copy-done.4
  78.7 1.5 %multiply_add_fusion = (f32[2,4,16,128]{3,2,1,0:T(8,128)}, f32[2,4,16,128]{3,2,1,0:T(8,128)}, f32[2,4,16,128]{3,2,1,0:T(8,128)}) fusion(f32[2,4,16,128]{3,2,1,0:T(8,128)S(1)} %copy-done, f32[128]{0:T(128)S(1)} %bitcast.7, f32[2,4,16,128]{3,2,1,0:T(8,128)S(1)} %copy-done.1, f32[2,4,16,128]{3,2,1,0:T(8,128)} %get-tuple-element.7, f32[128]{0:T(128)S(1)} %bitcast.6, ...), kind=kLoop, calls=%fused_computation | loop fusion | flops 98304 | bytes 459776 | tf_op jit(solution)/shard_map/add | solution.py:460
Async XLA Ops:
  0.6 77.4 %copy-start = (f32[2,4,16,128]{3,2,1,0:T(8,128)S(1)}, f32[2,4,16,128]{3,2,1,0:T(8,128)}, u32[]{:S(2)}) copy-start(f32[2,4,16,128]{3,2,1,0:T(8,128)} %p_hbm.1) | copy-start | bytes 196612
  0.6 77.4 %copy-start.1 = (f32[2,4,16,128]{3,2,1,0:T(8,128)S(1)}, f32[2,4,16,128]{3,2,1,0:T(8,128)}, u32[]{:S(2)}) copy-start(f32[2,4,16,128]{3,2,1,0:T(8,128)} %r_hbm.1) | copy-start | bytes 196612
  0.7 77.4 %copy-start.2 = (f32[2,4,16,128]{3,2,1,0:T(8,128)S(1)}, f32[2,4,16,128]{3,2,1,0:T(8,128)}, u32[]{:S(2)}) copy-start(f32[2,4,16,128]{3,2,1,0:T(8,128)} %param.9) | copy-start | bytes 196612
  78.0 0.6 copy-start.3
  78.0 0.7 copy-start.4

commit v2 on v1

--- a/solution.py
+++ b/solution.py
@@ -27,8 +27,9 @@
     cos, sin = np.cos(angle) / math.sqrt(N), np.sin(angle) / math.sqrt(N)
     left = np.block([[cos, sin], [-sin, cos]])
     order = [c * N + 4 * t + i for t in range(NT) for c in range(2) for i in range(4)]
+    leave = [c * N + 4 * t + 2 * p + i for p in range(2) for t in range(NT) for c in range(2) for i in range(2)]
     out = []
-    for table in (left, left.T, left[:, order], left[:, order].T):
+    for table in (left, left.T, left[:, order], left[:, leave].T):
         table = table.astype(np.float32)
         high = table.astype(ml_dtypes.bfloat16)
         low = (table - high.astype(np.float32)).astype(ml_dtypes.bfloat16)
@@ -59,7 +60,7 @@
     tab, smap, kb, rv, pbuf, wsend, wbuf, onehot, pt, pi,
     send1, recv1, boxes, placed, send2, recv2, rs_send, rs_near, rs_sum, rs_recv,
     nv, alphas, betas, ar1, ar1c, ar1z, ar1y, ar2, ar2c, ar2z, ar2y,
-    load_sem, loc_sem, ag_s, ag_r, agf_s, agf_r, w1_s, w1_r, a1_s, a1_r, a2_s, a2_r, w2f_s, w2f_r, w2_s, w2_r,
+    load_sem, loc_sem, ag_s, ag_r, agf_s, agf_r, w1_s, w1_r, a1_s, a1_r, w2f_s, w2f_r, w2_s, w2_r, a2_s, a2_r,
     rn_s, rn_r, rs_s, rs_r, r1_s, r1_r, r2_s, r2_r, out_sem,
 ):
     ci, ti = lax.axis_index("coil"), lax.axis_index("tile")
@@ -172,14 +173,14 @@
 
     own_w = pltpu.make_async_copy(wsend.at[pl.ds(pl.multiple_of(ti * 8, 8), 8)], wbuf.at[ci, ti], loc_sem.at[0])
     own_w.start()
-    send_weights(0, 16)
+    send_weights(0, 20)
     for k in (1, 3, 2):
         came = pbuf.at[chip(4 - k)]
         await_bytes(came, ag_r.at[k - 1])
         push(came, came, (agf_s, agf_r), (near, ti))
         if k == 3:
-            send_weights(16, 24)
-    send_weights(24, NT - 1)
+            send_weights(20, 25)
+    send_weights(25, NT - 1)
 
     sub16 = lax.broadcasted_iota(I32, (16, 2 * N), 0)
     lane16 = lax.broadcasted_iota(I32, (16, 2 * N), 1)
@@ -233,11 +234,15 @@
     def rows_of(t):
         return pl.ds(pl.multiple_of(t * 32, 32), 32)
 
+    def send_1(t):
+        push(send1.at[rows_of(t)], recv1.at[ti], (a1_s, a1_r), (ci, t))
+
+    tiles(send_1, 0, 14)
     own_w.wait()
     await_bytes(wbuf.at[ci, pl.ds(0, NT - 1)], w1_r)
     for k in (2, 1, 3):
         push(wbuf.at[ci], wbuf.at[ci], (w2_s.at[k - 1], w2_r.at[k - 1]), (chip(k), ti))
-    tiles(lambda t: push(send1.at[rows_of(t)], recv1.at[ti], (a1_s, a1_r), (ci, t)))
+    tiles(send_1, 14)
     own_1 = pltpu.make_async_copy(send1.at[rows_of(ti)], recv1.at[ti], loc_sem.at[1])
     own_1.start()
 
@@ -254,14 +259,7 @@
     await_bytes(recv1.at[pl.ds(0, NT - 1)], a1_r)
     for e in range(0, 4, 2):
         got = [recv1[:, (e + i) * 8 : (e + i + 1) * 8, :].reshape(2 * N, N) for i in range(2)]
-        field = split(jnp.concatenate(got, axis=1))
-
-        def cut(g, carry, e=e, field=field):
-            rows = pl.ds(pl.multiple_of(g * 256, 256), 256)
-            boxes[rows, e * N : (e + 2) * N] = dot3((pt[0, rows, :], pt[1, rows, :]), field)
-            return carry
-
-        lax.fori_loop(0, 4, cut, 0)
+        boxes[:, e * N : (e + 2) * N] = dot3((pt[0], pt[1]), split(jnp.concatenate(got, axis=1)))
 
     await_bytes(wbuf.at[pl.ds(0, 4)], w2f_r)
     lane8 = lax.broadcasted_iota(I32, (8, N), 1)
@@ -318,26 +316,43 @@
     first_sum = Sum(both, ar1, (ar1c, ar1z, ar1y), (r1_s, r1_r))
     first_sum.send()
 
-    for e in range(0, 4, 2):
-        columns = slice(e * N, (e + 2) * N)
+    low = lax.rem(lax.broadcasted_iota(I32, (2 * N, N), 0), 8) < 4
+    for e in range(2):
+        columns = slice(2 * e * N, (2 * e + 2) * N)
         back = dot3((pi[0], pi[1]), (placed[0, :, columns], placed[1, :, columns]))
-        for i in range(2):
-            send2[:, (e + i) * 8 : (e + i + 1) * 8, :] = back[:, i * N : (i + 1) * N].reshape(NT, 8, N)
+        one, two = back[:, :N], back[:, N:]
+        even = jnp.where(low, one, pltpu.roll(two, 4, 0))
+        odd = jnp.where(low, pltpu.roll(one, 2 * N - 4, 0), two)
+        send2[:, :, 0, e * 8 : (e + 1) * 8, :] = even.reshape(2, NT // 2, 8, N)
+        send2[:, :, 1, e * 8 : (e + 1) * 8, :] = odd.reshape(2, NT // 2, 8, N)
+
+    def place_of(t):
+        return pl.ds(pl.multiple_of(t * 16, 16), 16)
+
+    owns = []
+    for pair in range(2):
+        tiles(lambda t, pair=pair: push(
+            send2.at[pair, t // 2, lax.rem(t, 2)], recv2.at[pair, place_of(ti)],
+            (a2_s.at[pair], a2_r.at[pair]), (ci, t)))
+        owns.append(pltpu.make_async_copy(
+            send2.at[pair, ti // 2, lax.rem(ti, 2)], recv2.at[pair, place_of(ti)], loc_sem.at[2 + pair]))
+        owns[pair].start()
     first_sum.take()
     first_sum.send()
 
-    tiles(lambda t: push(send2.at[t], recv2.at[rows_of(ti)], (a2_s, a2_r), (ci, t)))
-    own_2 = pltpu.make_async_copy(send2.at[ti], recv2.at[rows_of(ti)], loc_sem.at[2])
-    own_2.start()
-
-    first_sum.take()
-    first_sum.send()
-
-    own_2.wait()
-    await_bytes(recv1.at[pl.ds(0, NT - 1)], a2_r)
+    def spread_sum(pair):
+        await_bytes(rs_near.at[pair], rn_r.at[pair])
+        rs_sum[pair] = rs_send[core, pair] + rs_near[pair]
+        for k in (2, 1, 3):
+            to = lax.rem(cx + k, 4)
+            push(rs_sum.at[pair, to], rs_recv.at[pair, cx], (rs_s.at[pair], rs_r.at[pair]), (chip(k), ti))
+        rs_recv[pair, cx] = rs_sum[pair, cx]
+
     for pair in range(2):
+        owns[pair].wait()
+        await_bytes(recv2.at[pair, pl.ds(0, 16 * (NT - 1))], a2_r.at[pair])
         columns = [
-            jnp.concatenate([recv2[pl.ds(c * 4 + 2 * pair + i, N, stride=8), :] for c in range(2)], axis=0)
+            jnp.concatenate([recv2[pair, pl.ds(c * 2 + i, N, stride=4), :] for c in range(2)], axis=0)
             for i in range(2)
         ]
         along_y = dot3(right, split(jnp.concatenate(columns, axis=1)))
@@ -355,14 +370,11 @@
                 for half in range(2):
                     rs_send[half, pair, :, c, i] = back[:, half]
         push(rs_send.at[1 - core, pair], rs_near.at[pair], (rn_s.at[pair], rn_r.at[pair]), (near, ti))
-
-    for pair in range(2):
-        await_bytes(rs_near.at[pair], rn_r.at[pair])
-        rs_sum[pair] = rs_send[core, pair] + rs_near[pair]
-        for k in (2, 1, 3):
-            to = lax.rem(cx + k, 4)
-            push(rs_sum.at[pair, to], rs_recv.at[pair, cx], (rs_s.at[pair], rs_r.at[pair]), (chip(k), ti))
-        rs_recv[pair, cx] = rs_sum[pair, cx]
+        if pair == 0:
+            spread_sum(0)
+            first_sum.take()
+            first_sum.send()
+    spread_sum(1)
     sums = jnp.sum(first_sum.take(), axis=1, keepdims=True)
     norm_now, product = sums[0:1], sums[1:2]
     alpha = norm_now / product
@@ -397,8 +409,8 @@
         await_bytes(wbuf.at[0], w2_s.at[k])
     await_bytes(wbuf.at[pl.ds(0, 4)], w2f_s)
     await_bytes(recv1.at[pl.ds(0, NT - 1)], a1_s)
-    await_bytes(recv1.at[pl.ds(0, NT - 1)], a2_s)
     for pair in range(2):
+        await_bytes(recv2.at[pair, pl.ds(0, 16 * (NT - 1))], a2_s.at[pair])
         await_bytes(rs_near.at[pair], rn_s.at[pair])
         await_bytes(rs_recv.at[pair, pl.ds(0, 3)], rs_s.at[pair])
     first_sum.sent()
@@ -427,8 +439,8 @@
         vmem((NT, 32, N), F32),
         vmem((8 * N, 4 * N), F32),
         vmem((2, 8 * N, 4 * N), BF16),
-        vmem((NT, 32, N), F32),
-        vmem((8 * N, N), F32),
+        vmem((2, NT // 2, 2, 16, N), F32),
+        vmem((2, 4 * N, N), F32),
         vmem((2, 2, 4, 2, 2, 16, N), F32),
         vmem((2, 4, 2, 2, 16, N), F32),
         vmem((2, 4, 2, 2, 16, N), F32),
@@ -439,8 +451,8 @@
     ]
     for _ in range(2):
         scratch += [vmem((3, 8, N), F32)] + [vmem((n, 8, N), F32) for n in (NC, 8, 4)]
-    scratch += [dma((n,)) for n in (5, 3, 3, 3)] + [dma(())] * 10
-    scratch += [dma((3,))] * 2 + [dma((2,))] * 4 + [dma((3,))] * 5
+    scratch += [dma((n,)) for n in (5, 4, 3, 3)] + [dma(())] * 8
+    scratch += [dma((3,))] * 2 + [dma((2,))] * 6 + [dma((3,))] * 5
     step = jax.ShapeDtypeStruct((1, 1, 1, N), F32)
     normal, alpha, beta = pl.pallas_call(
         kernel,

time: 80.4 us -> 72.5 us (0.902)
  Pallas kernels: 77.3 us -> 69.4 us
    pallas_call x1, Pallas kernels: 77.3 us -> 69.4 us  [shards(): pl.pallas_call(kernel, out_shape=(jax.ShapeDtypeStruct(shard, F32), step,...]
where the time goes in v2:
time: 72.5 us; the launch traced here: 72.3 us
  Pallas kernels  69.4 us (96%)
  other arithmetic  1.53 us (2%)
    pallas_call x1, Pallas kernels, shards(): pl.pallas_call(kernel, out_shape=(jax.ShapeDtypeStruct(shard, F32), step,...  69.4 us
    add x1, other arithmetic, shards(): next_p = next_r + beta * image_p  1.53 us

profile of v2, /device:TPU:1, one launch (start us, length us, event | category | flops | bytes accessed | tf_op | source)
XLA Modules:
  0.0 72.3 jit_solution(14693704437271436369)
XLA Ops:
  0.6 0.0 copy-start
  0.6 0.0 copy-start.1
  0.7 0.0 copy-start.2
  0.7 69.4 %shard_map.103 = (f32[2,4,16,128]{3,2,1,0:T(8,128)}, f32[1,1,1,128]{3,2,1,0:T(1,128)}, f32[1,1,1,128]{3,2,1,0:T(1,128)}) custom-call(f32[2,4,16,128]{3,2,1,0:T(8,128)} %p_hbm.1, f32[2,4,16,128]{3,2,1,0:T(8,128)} %r_hbm.1, f32[1,2,4,128,128]{4,3,2,1,0:T(8,128)} %s_hbm.1, f32[384,128]{1,0:T(8,128)} %bitcast.4, s32[32]{0:T(128)} %own.1, ...), custom_call_target="tpu_custom_call" | custom-call | tf_op jit(solution)/shard_map/pallas_call | solution.py:457
  70.1 0.0 copy-start.3
  70.1 0.0 copy-start.4
  70.1 0.0 copy-done
  70.1 0.0 copy-done.1
  70.1 0.0 copy-done.2
  70.1 0.6 copy-done.3
  70.7 0.1 copy-done.4
  70.7 1.5 %multiply_add_fusion = (f32[2,4,16,128]{3,2,1,0:T(8,128)}, f32[2,4,16,128]{3,2,1,0:T(8,128)}, f32[2,4,16,128]{3,2,1,0:T(8,128)}) fusion(f32[2,4,16,128]{3,2,1,0:T(8,128)S(1)} %copy-done, f32[128]{0:T(128)S(1)} %bitcast.7, f32[2,4,16,128]{3,2,1,0:T(8,128)S(1)} %copy-done.1, f32[2,4,16,128]{3,2,1,0:T(8,128)} %get-tuple-element.7, f32[128]{0:T(128)S(1)} %bitcast.6, ...), kind=kLoop, calls=%fused_computation | loop fusion | flops 98304 | bytes 459776 | tf_op jit(solution)/shard_map/add | solution.py:472
Async XLA Ops:
  0.6 69.5 %copy-start = (f32[2,4,16,128]{3,2,1,0:T(8,128)S(1)}, f32[2,4,16,128]{3,2,1,0:T(8,128)}, u32[]{:S(2)}) copy-start(f32[2,4,16,128]{3,2,1,0:T(8,128)} %p_hbm.1) | copy-start | bytes 196612
  0.6 69.5 %copy-start.1 = (f32[2,4,16,128]{3,2,1,0:T(8,128)S(1)}, f32[2,4,16,128]{3,2,1,0:T(8,128)}, u32[]{:S(2)}) copy-start(f32[2,4,16,128]{3,2,1,0:T(8,128)} %r_hbm.1) | copy-start | bytes 196612
  0.7 69.5 %copy-start.2 = (f32[2,4,16,128]{3,2,1,0:T(8,128)S(1)}, f32[2,4,16,128]{3,2,1,0:T(8,128)}, u32[]{:S(2)}) copy-start(f32[2,4,16,128]{3,2,1,0:T(8,128)} %param.9) | copy-start | bytes 196612
  70.1 0.6 copy-start.3
  70.1 0.7 copy-start.4

commit v3 on v2

--- a/solution.py
+++ b/solution.py
@@ -59,7 +59,7 @@
     normal_hbm, alpha_hbm, beta_hbm,
     tab, smap, kb, rv, pbuf, wsend, wbuf, onehot, pt, pi,
     send1, recv1, boxes, placed, send2, recv2, rs_send, rs_near, rs_sum, rs_recv,
-    nv, alphas, betas, ar1, ar1c, ar1z, ar1y, ar2, ar2c, ar2z, ar2y,
+    nv, alphas, betas, ar1, ar1c, ar1z, ar1y, ar2, ar2a, ar2b,
     load_sem, loc_sem, ag_s, ag_r, agf_s, agf_r, w1_s, w1_r, a1_s, a1_r, w2f_s, w2f_r, w2_s, w2_r, a2_s, a2_r,
     rn_s, rn_r, rs_s, rs_r, r1_s, r1_r, r2_s, r2_r, out_sem,
 ):
@@ -101,6 +101,14 @@
     barrier = pltpu.get_barrier_semaphore()
     tiles(lambda t: pl.semaphore_signal(barrier, inc=1, device_id=(ci, t), device_id_type=MESH))
     ring(ci, NC, lambda c: pl.semaphore_signal(barrier, inc=1, device_id=(c, ti), device_id_type=MESH))
+
+    def greet(count, device):
+        def step(i, carry):
+            pl.semaphore_signal(barrier, inc=1, device_id=device(i), device_id_type=MESH)
+            return carry
+
+        lax.fori_loop(0, count, step, 0)
+
     for load in loads:
         load.start()
 
@@ -113,18 +121,27 @@
     def await_bytes(ref, sem):
         pltpu.make_async_copy(ref, ref, sem).wait()
 
+    over_coil = (NC, ci, lambda i: (partner(ci, NC, i), ti))
+    over_z = (8, z, lambda i: (ci, partner(z, 8, i) * 4 + y))
+    over_y = (4, y, lambda i: (ci, z * 4 + partner(y, 4, i)))
+    over_tile = (32, ti, lambda i: (ci, partner(z, 8, lax.rem(i, 8)) * 4 + partner(y, 4, i // 8)))
+
     class Sum:
-        def __init__(self, part, held, slots, sems):
-            self.part, self.held, self.slots, self.sems, self.stage = part, held, slots, sems, 0
+        def __init__(self, part, stages, held, slots, sems):
+            self.part, self.stages, self.held, self.slots, self.sems, self.stage = part, stages, held, slots, sems, 0
 
         def send(self):
             stage = self.stage
             slot, sems = self.slots[stage], (self.sems[0].at[stage], self.sems[1].at[stage])
             self.held[stage] = self.part
             src = self.held.at[stage]
-            me = (ci, z, y)[stage]
-            device = (lambda i: (i, ti), lambda i: (ci, i * 4 + y), lambda i: (ci, z * 4 + i))[stage]
-            ring(me, slot.shape[0], lambda i: push(src, slot.at[me], sems, device(i)))
+            size, me, device = self.stages[stage]
+
+            def step(i, carry):
+                push(src, slot.at[me], sems, device(i))
+                return carry
+
+            lax.fori_loop(0, size - 1, step, 0)
             slot[me] = self.part
 
         def take(self):
@@ -173,14 +190,14 @@
 
     own_w = pltpu.make_async_copy(wsend.at[pl.ds(pl.multiple_of(ti * 8, 8), 8)], wbuf.at[ci, ti], loc_sem.at[0])
     own_w.start()
-    send_weights(0, 20)
+    send_weights(0, 14)
     for k in (1, 3, 2):
         came = pbuf.at[chip(4 - k)]
         await_bytes(came, ag_r.at[k - 1])
         push(came, came, (agf_s, agf_r), (near, ti))
         if k == 3:
-            send_weights(20, 25)
-    send_weights(25, NT - 1)
+            send_weights(14, 21)
+    send_weights(21, NT - 1)
 
     sub16 = lax.broadcasted_iota(I32, (16, 2 * N), 0)
     lane16 = lax.broadcasted_iota(I32, (16, 2 * N), 1)
@@ -207,7 +224,7 @@
     for i in range(2):
         for g in range(4):
             columns = slice(g * 256, (g + 1) * 256)
-            pi[i, :, columns] = dot_t(tab[6 + i], onehot[columns, :]).astype(BF16)
+            pi[i * 2 * N : (i + 1) * 2 * N, columns] = dot_t(tab[6 + i], onehot[columns, :]).astype(BF16)
 
     loads[2].wait()
     await_bytes(pbuf.at[pl.ds(0, 4)], agf_r)
@@ -307,19 +324,19 @@
             placed[1, rows, e * N : (e + 1) * N] = low
         return total
 
-    product_part = lax.fori_loop(0, NT // 2, regrid, jnp.zeros((8, N), F32), unroll=4) * 0.25
+    product_part = lax.fori_loop(0, NT // 2, regrid, jnp.zeros((8, N), F32), unroll=16) * 0.25
 
     row8 = lax.broadcasted_iota(I32, (8, N), 0)
     norm_row = jnp.sum(norm_part, axis=0, keepdims=True)
     product_row = jnp.sum(product_part, axis=0, keepdims=True)
     both = jnp.where(row8 == 0, norm_row, jnp.where(row8 == 1, product_row, 0.0))
-    first_sum = Sum(both, ar1, (ar1c, ar1z, ar1y), (r1_s, r1_r))
-    first_sum.send()
+    first_sum = Sum(both, (over_coil, over_z, over_y), ar1, (ar1c, ar1z, ar1y), (r1_s, r1_r))
 
     low = lax.rem(lax.broadcasted_iota(I32, (2 * N, N), 0), 8) < 4
     for e in range(2):
         columns = slice(2 * e * N, (2 * e + 2) * N)
-        back = dot3((pi[0], pi[1]), (placed[0, :, columns], placed[1, :, columns]))
+        both_terms = dot(pi[...], placed[0, :, columns])
+        back = both_terms[: 2 * N] + (both_terms[2 * N :] + dot(pi[: 2 * N], placed[1, :, columns]))
         one, two = back[:, :N], back[:, N:]
         even = jnp.where(low, one, pltpu.roll(two, 4, 0))
         odd = jnp.where(low, pltpu.roll(one, 2 * N - 4, 0), two)
@@ -337,6 +354,8 @@
         owns.append(pltpu.make_async_copy(
             send2.at[pair, ti // 2, lax.rem(ti, 2)], recv2.at[pair, place_of(ti)], loc_sem.at[2 + pair]))
         owns[pair].start()
+        if pair == 0:
+            first_sum.send()
     first_sum.take()
     first_sum.send()
 
@@ -392,8 +411,8 @@
     out_a = pltpu.make_async_copy(alphas, alpha_hbm, out_sem.at[1])
     out_a.start()
 
-    last_sum = Sum(norm_next, ar2, (ar2c, ar2z, ar2y), (r2_s, r2_r))
-    for _ in range(3):
+    last_sum = Sum(norm_next, (over_coil, over_tile), ar2, (ar2a, ar2b), (r2_s, r2_r))
+    for _ in range(2):
         last_sum.send()
         sums = last_sum.take()
     sums = jnp.sum(jnp.sum(sums, axis=0, keepdims=True), axis=1, keepdims=True)
@@ -434,7 +453,7 @@
         vmem((NC, NT, 8, N), F32),
         vmem((8 * N, 2 * N), BF16),
         vmem((2, 8 * N, 2 * N), BF16),
-        vmem((2, 2 * N, 8 * N), BF16),
+        vmem((4 * N, 8 * N), BF16),
         vmem((8 * N, N), F32),
         vmem((NT, 32, N), F32),
         vmem((8 * N, 4 * N), F32),
@@ -449,8 +468,8 @@
         vmem((1, 1, 1, N), F32),
         vmem((1, 1, 1, N), F32),
     ]
-    for _ in range(2):
-        scratch += [vmem((3, 8, N), F32)] + [vmem((n, 8, N), F32) for n in (NC, 8, 4)]
+    for sizes in ((NC, 8, 4), (NC, NT)):
+        scratch += [vmem((len(sizes), 8, N), F32)] + [vmem((n, 8, N), F32) for n in sizes]
     scratch += [dma((n,)) for n in (5, 4, 3, 3)] + [dma(())] * 8
     scratch += [dma((3,))] * 2 + [dma((2,))] * 6 + [dma((3,))] * 5
     step = jax.ShapeDtypeStruct((1, 1, 1, N), F32)

time: 72.5 us -> 70.1 us (0.967)
  Pallas kernels: 69.4 us -> 67.1 us
    pallas_call x1, Pallas kernels: 69.4 us -> 67.1 us  [shards(): pl.pallas_call(kernel, out_shape=(jax.ShapeDtypeStruct(shard, F32), step,...]
where the time goes in v3:
time: 70.1 us; the launch traced here: 69.9 us
  Pallas kernels  67.1 us (96%)
  other arithmetic  1.53 us (2%)
    pallas_call x1, Pallas kernels, shards(): pl.pallas_call(kernel, out_shape=(jax.ShapeDtypeStruct(shard, F32), step,...  67.1 us
    add x1, other arithmetic, shards(): next_p = next_r + beta * image_p  1.53 us

profile of v3, /device:TPU:1, one launch (start us, length us, event | category | flops | bytes accessed | tf_op | source)
XLA Modules:
  0.0 69.9 jit_solution(13603683385788189100)
XLA Ops:
  0.6 0.0 copy-start
  0.6 0.0 copy-start.1
  0.7 0.0 copy-start.2
  0.7 67.1 %shard_map.103 = (f32[2,4,16,128]{3,2,1,0:T(8,128)}, f32[1,1,1,128]{3,2,1,0:T(1,128)}, f32[1,1,1,128]{3,2,1,0:T(1,128)}) custom-call(f32[2,4,16,128]{3,2,1,0:T(8,128)} %p_hbm.1, f32[2,4,16,128]{3,2,1,0:T(8,128)} %r_hbm.1, f32[1,2,4,128,128]{4,3,2,1,0:T(8,128)} %s_hbm.1, f32[384,128]{1,0:T(8,128)} %bitcast.4, s32[32]{0:T(128)} %own.1, ...), custom_call_target="tpu_custom_call" | custom-call | tf_op jit(solution)/shard_map/pallas_call | solution.py:476
  67.7 0.0 copy-start.3
  67.7 0.0 copy-start.4
  67.8 0.0 copy-done
  67.8 0.0 copy-done.1
  67.8 0.0 copy-done.2
  67.8 0.6 copy-done.3
  68.4 0.1 copy-done.4
  68.4 1.5 %multiply_add_fusion = (f32[2,4,16,128]{3,2,1,0:T(8,128)}, f32[2,4,16,128]{3,2,1,0:T(8,128)}, f32[2,4,16,128]{3,2,1,0:T(8,128)}) fusion(f32[2,4,16,128]{3,2,1,0:T(8,128)S(1)} %copy-done, f32[128]{0:T(128)S(1)} %bitcast.7, f32[2,4,16,128]{3,2,1,0:T(8,128)S(1)} %copy-done.1, f32[2,4,16,128]{3,2,1,0:T(8,128)} %get-tuple-element.7, f32[128]{0:T(128)S(1)} %bitcast.6, ...), kind=kLoop, calls=%fused_computation | loop fusion | flops 98304 | bytes 459776 | tf_op jit(solution)/shard_map/add | solution.py:491
Async XLA Ops:
  0.6 67.1 %copy-start = (f32[2,4,16,128]{3,2,1,0:T(8,128)S(1)}, f32[2,4,16,128]{3,2,1,0:T(8,128)}, u32[]{:S(2)}) copy-start(f32[2,4,16,128]{3,2,1,0:T(8,128)} %p_hbm.1) | copy-start | bytes 196612
  0.6 67.1 %copy-start.1 = (f32[2,4,16,128]{3,2,1,0:T(8,128)S(1)}, f32[2,4,16,128]{3,2,1,0:T(8,128)}, u32[]{:S(2)}) copy-start(f32[2,4,16,128]{3,2,1,0:T(8,128)} %r_hbm.1) | copy-start | bytes 196612
  0.7 67.1 %copy-start.2 = (f32[2,4,16,128]{3,2,1,0:T(8,128)S(1)}, f32[2,4,16,128]{3,2,1,0:T(8,128)}, u32[]{:S(2)}) copy-start(f32[2,4,16,128]{3,2,1,0:T(8,128)} %param.9) | copy-start | bytes 196612
  67.7 0.6 copy-start.3
  67.7 0.7 copy-start.4

commit v4 on v3

--- a/solution.py
+++ b/solution.py
@@ -26,10 +26,9 @@
     angle = 2.0 * math.pi / N * ((cells[:, None] * cells[None, :]) % N)
     cos, sin = np.cos(angle) / math.sqrt(N), np.sin(angle) / math.sqrt(N)
     left = np.block([[cos, sin], [-sin, cos]])
-    order = [c * N + 4 * t + i for t in range(NT) for c in range(2) for i in range(4)]
-    leave = [c * N + 4 * t + 2 * p + i for p in range(2) for t in range(NT) for c in range(2) for i in range(2)]
+    order = [c * N + 4 * t + 2 * p + i for p in range(2) for t in range(NT) for c in range(2) for i in range(2)]
     out = []
-    for table in (left, left.T, left[:, order], left[:, leave].T):
+    for table in (left, left.T, left[:, order], left[:, order].T):
         table = table.astype(np.float32)
         high = table.astype(ml_dtypes.bfloat16)
         low = (table - high.astype(np.float32)).astype(ml_dtypes.bfloat16)
@@ -179,10 +178,15 @@
         return lax.rem(ci + 2 * k, NC)
 
     loads[3].wait()
-    mine = pbuf.at[ci]
-    for k in (2, 1, 3):
-        push(mine, mine, (ag_s.at[k - 1], ag_r.at[k - 1]), (chip(k), ti))
-    push(mine, mine, (agf_s, agf_r), (near, ti))
+
+    def half_of(c, pair):
+        return pbuf.at[c, :, pl.ds(2 * pair, 2)]
+
+    for pair in range(2):
+        mine = half_of(ci, pair)
+        for k in (2, 1, 3):
+            push(mine, mine, (ag_s.at[3 * pair + k - 1], ag_r.at[3 * pair + k - 1]), (chip(k), ti))
+        push(mine, mine, (agf_s.at[pair], agf_r.at[pair]), (near, ti))
 
     def send_weights(first, last):
         tiles(lambda t: push(
@@ -190,46 +194,38 @@
 
     own_w = pltpu.make_async_copy(wsend.at[pl.ds(pl.multiple_of(ti * 8, 8), 8)], wbuf.at[ci, ti], loc_sem.at[0])
     own_w.start()
-    send_weights(0, 14)
+    def forward(pair, k):
+        came = half_of(chip(4 - k), pair)
+        await_bytes(came, ag_r.at[3 * pair + k - 1])
+        push(came, came, (agf_s.at[pair], agf_r.at[pair]), (near, ti))
+
+    send_weights(0, 8)
+    forward(0, 1)
+    forward(0, 3)
+    send_weights(8, 12)
+    forward(0, 2)
+    send_weights(12, 18)
     for k in (1, 3, 2):
-        came = pbuf.at[chip(4 - k)]
-        await_bytes(came, ag_r.at[k - 1])
-        push(came, came, (agf_s, agf_r), (near, ti))
-        if k == 3:
-            send_weights(14, 21)
-    send_weights(21, NT - 1)
-
-    sub16 = lax.broadcasted_iota(I32, (16, 2 * N), 0)
-    lane16 = lax.broadcasted_iota(I32, (16, 2 * N), 1)
-    base16 = (sub16 & 1) * N + ((sub16 >> 1) & 3)
-
-    def mark(h, carry):
-        for half in range(2):
-            start = jnp.where(sub16 < 8, offs[0, 0, 2 * half, h], offs[0, 0, 2 * half + 1, h])
-            hit = jnp.where(lane16 == base16 + start, 1.0, 0.0).astype(BF16)
-            onehot[pl.ds(pl.multiple_of(h * 32 + half * 16, 16), 16), :] = hit
-        return carry
-
-    lax.fori_loop(0, NT, mark, 0)
+        forward(1, k)
+    send_weights(18, NT - 1)
+
     loads[1].wait()
-
-    def phases(g, carry):
-        rows = pl.ds(pl.multiple_of(g * 256, 256), 256)
-        hot = onehot[rows, :]
-        for i in range(2):
-            pt[i, rows, :] = dot(hot, tab[4 + i]).astype(BF16)
-        return carry
-
-    lax.fori_loop(0, 4, phases, 0)
-    for i in range(2):
-        for g in range(4):
-            columns = slice(g * 256, (g + 1) * 256)
-            pi[i * 2 * N : (i + 1) * 2 * N, columns] = dot_t(tab[6 + i], onehot[columns, :]).astype(BF16)
-
     loads[2].wait()
-    await_bytes(pbuf.at[pl.ds(0, 4)], agf_r)
     left, right = (tab[0], tab[1]), (tab[2], tab[3])
-    for pair in range(2):
+
+    def place_of(t):
+        return pl.ds(pl.multiple_of(t * 16, 16), 16)
+
+    def share_weights():
+        own_w.wait()
+        await_bytes(wbuf.at[ci, pl.ds(0, NT - 1)], w1_r)
+        for k in (2, 1, 3):
+            push(wbuf.at[ci], wbuf.at[ci], (w2_s.at[k - 1], w2_r.at[k - 1]), (chip(k), ti))
+        push(wbuf.at[ci], wbuf.at[ci], (w2f_s, w2f_r), (near, ti))
+
+    own_1 = []
+    for pair in range(2):
+        await_bytes(pbuf.at[pl.ds(0, 4), :, pl.ds(0, 2)], agf_r.at[pair])
         parts = []
         for xi in (2 * pair, 2 * pair + 1):
             p_re = pbuf[:, 0, xi].reshape(N, N)
@@ -244,39 +240,67 @@
         along_y = dot3(left, split(jnp.concatenate(columns, axis=1)))
         for i in range(2):
             for c in range(2):
-                send1[pl.ds(c * 4 + 2 * pair + i, N, stride=8), :] = along_y[
-                    c * N : (c + 1) * N, i * N : (i + 1) * N
-                ]
-
-    def rows_of(t):
-        return pl.ds(pl.multiple_of(t * 32, 32), 32)
-
-    def send_1(t):
-        push(send1.at[rows_of(t)], recv1.at[ti], (a1_s, a1_r), (ci, t))
-
-    tiles(send_1, 0, 14)
-    own_w.wait()
-    await_bytes(wbuf.at[ci, pl.ds(0, NT - 1)], w1_r)
-    for k in (2, 1, 3):
-        push(wbuf.at[ci], wbuf.at[ci], (w2_s.at[k - 1], w2_r.at[k - 1]), (chip(k), ti))
-    tiles(send_1, 14)
-    own_1 = pltpu.make_async_copy(send1.at[rows_of(ti)], recv1.at[ti], loc_sem.at[1])
-    own_1.start()
-
-    push(wbuf.at[ci], wbuf.at[ci], (w2f_s, w2f_r), (near, ti))
+                send1[pair, pl.ds(c * 2 + i, N, stride=4), :] = along_y[c * N : (c + 1) * N, i * N : (i + 1) * N]
+
+        def send_1(t, pair=pair):
+            push(
+                send1.at[pair, place_of(t)], recv1.at[pair, ti // 2, lax.rem(ti, 2)],
+                (a1_s.at[pair], a1_r.at[pair]), (ci, t))
+
+        if pair == 0:
+            tiles(send_1, 0, 10)
+            share_weights()
+            tiles(send_1, 10)
+        else:
+            tiles(send_1)
+        own_1.append(pltpu.make_async_copy(
+            send1.at[pair, place_of(ti)], recv1.at[pair, ti // 2, lax.rem(ti, 2)], loc_sem.at[1 + 3 * pair]))
+        own_1[pair].start()
+
     for k in (1, 3, 2):
         came = wbuf.at[chip(4 - k)]
         await_bytes(came, w2_r.at[k - 1])
         push(came, came, (w2f_s, w2f_r), (near, ti))
 
+    sub16 = lax.broadcasted_iota(I32, (16, 2 * N), 0)
+    lane16 = lax.broadcasted_iota(I32, (16, 2 * N), 1)
+    base16 = (sub16 & 1) * N + ((sub16 >> 1) & 3)
+
+    def mark(h, carry):
+        for half in range(2):
+            start = jnp.where(sub16 < 8, offs[0, 0, 2 * half, h], offs[0, 0, 2 * half + 1, h])
+            hit = jnp.where(lane16 == base16 + start, 1.0, 0.0).astype(BF16)
+            onehot[pl.ds(pl.multiple_of(h * 32 + half * 16, 16), 16), :] = hit
+        return carry
+
+    lax.fori_loop(0, NT, mark, 0)
+
+    def phases(g, carry):
+        rows = pl.ds(pl.multiple_of(g * 256, 256), 256)
+        hot = onehot[rows, :]
+        for i in range(2):
+            pt[i, rows, :] = dot(hot, tab[4 + i]).astype(BF16)
+        return carry
+
+    lax.fori_loop(0, 4, phases, 0)
+    for i in range(2):
+        for g in range(4):
+            columns = slice(g * 256, (g + 1) * 256)
+            pi[i * 2 * N : (i + 1) * 2 * N, columns] = dot_t(tab[6 + i], onehot[columns, :]).astype(BF16)
+
     loads[4].wait()
     norm_part = jnp.sum(rv[...].reshape(16, 8, N) * rv[...].reshape(16, 8, N), axis=0)
 
-    own_1.wait()
-    await_bytes(recv1.at[pl.ds(0, NT - 1)], a1_r)
-    for e in range(0, 4, 2):
-        got = [recv1[:, (e + i) * 8 : (e + i + 1) * 8, :].reshape(2 * N, N) for i in range(2)]
-        boxes[:, e * N : (e + 2) * N] = dot3((pt[0], pt[1]), split(jnp.concatenate(got, axis=1)))
+    for pair in range(2):
+        own_1[pair].wait()
+        await_bytes(send1.at[pair, pl.ds(0, 16 * (NT - 1))], a1_r.at[pair])
+    low = lax.rem(lax.broadcasted_iota(I32, (2 * N, N), 0), 8) < 4
+    for e in range(2):
+        even = recv1[:, :, 0, e * 8 : (e + 1) * 8, :].reshape(2 * N, N)
+        odd = recv1[:, :, 1, e * 8 : (e + 1) * 8, :].reshape(2 * N, N)
+        one = jnp.where(low, even, pltpu.roll(odd, 4, 0))
+        two = jnp.where(low, pltpu.roll(even, 2 * N - 4, 0), odd)
+        boxes[:, 2 * e * N : (2 * e + 2) * N] = dot3((pt[0], pt[1]), split(jnp.concatenate([one, two], axis=1)))
 
     await_bytes(wbuf.at[pl.ds(0, 4)], w2f_r)
     lane8 = lax.broadcasted_iota(I32, (8, N), 1)
@@ -332,22 +356,18 @@
     both = jnp.where(row8 == 0, norm_row, jnp.where(row8 == 1, product_row, 0.0))
     first_sum = Sum(both, (over_coil, over_z, over_y), ar1, (ar1c, ar1z, ar1y), (r1_s, r1_r))
 
-    low = lax.rem(lax.broadcasted_iota(I32, (2 * N, N), 0), 8) < 4
-    for e in range(2):
-        columns = slice(2 * e * N, (2 * e + 2) * N)
-        both_terms = dot(pi[...], placed[0, :, columns])
-        back = both_terms[: 2 * N] + (both_terms[2 * N :] + dot(pi[: 2 * N], placed[1, :, columns]))
-        one, two = back[:, :N], back[:, N:]
-        even = jnp.where(low, one, pltpu.roll(two, 4, 0))
-        odd = jnp.where(low, pltpu.roll(one, 2 * N - 4, 0), two)
-        send2[:, :, 0, e * 8 : (e + 1) * 8, :] = even.reshape(2, NT // 2, 8, N)
-        send2[:, :, 1, e * 8 : (e + 1) * 8, :] = odd.reshape(2, NT // 2, 8, N)
-
-    def place_of(t):
-        return pl.ds(pl.multiple_of(t * 16, 16), 16)
-
     owns = []
     for pair in range(2):
+        half = jnp.concatenate([pi[pair * N : (pair + 1) * N], pi[(2 + pair) * N : (3 + pair) * N]], axis=0)
+        for e in range(2):
+            columns = slice(2 * e * N, (2 * e + 2) * N)
+            both_terms = dot(half, placed[0, :, columns])
+            back = both_terms[:N] + (both_terms[N:] + dot(half[:N], placed[1, :, columns]))
+            one, two = back[:, :N], back[:, N:]
+            even = jnp.where(low[:N], one, pltpu.roll(two, 4, 0))
+            odd = jnp.where(low[:N], pltpu.roll(one, N - 4, 0), two)
+            send2[pair, :, 0, e * 8 : (e + 1) * 8, :] = even.reshape(NT // 2, 8, N)
+            send2[pair, :, 1, e * 8 : (e + 1) * 8, :] = odd.reshape(NT // 2, 8, N)
         tiles(lambda t, pair=pair: push(
             send2.at[pair, t // 2, lax.rem(t, 2)], recv2.at[pair, place_of(ti)],
             (a2_s.at[pair], a2_r.at[pair]), (ci, t)))
@@ -420,14 +440,15 @@
     out_b = pltpu.make_async_copy(betas, beta_hbm, out_sem.at[2])
     out_b.start()
 
-    for k in range(3):
-        await_bytes(pbuf.at[0], ag_s.at[k])
-    await_bytes(pbuf.at[pl.ds(0, 4)], agf_s)
+    for i in range(6):
+        await_bytes(half_of(0, 0), ag_s.at[i])
+    for pair in range(2):
+        await_bytes(pbuf.at[pl.ds(0, 4), :, pl.ds(0, 2)], agf_s.at[pair])
+        await_bytes(send1.at[pair, pl.ds(0, 16 * (NT - 1))], a1_s.at[pair])
     await_bytes(wbuf.at[0, pl.ds(0, NT - 1)], w1_s)
     for k in range(3):
         await_bytes(wbuf.at[0], w2_s.at[k])
     await_bytes(wbuf.at[pl.ds(0, 4)], w2f_s)
-    await_bytes(recv1.at[pl.ds(0, NT - 1)], a1_s)
     for pair in range(2):
         await_bytes(recv2.at[pair, pl.ds(0, 16 * (NT - 1))], a2_s.at[pair])
         await_bytes(rs_near.at[pair], rn_s.at[pair])
@@ -454,8 +475,8 @@
         vmem((8 * N, 2 * N), BF16),
         vmem((2, 8 * N, 2 * N), BF16),
         vmem((4 * N, 8 * N), BF16),
-        vmem((8 * N, N), F32),
-        vmem((NT, 32, N), F32),
+        vmem((2, 4 * N, N), F32),
+        vmem((2, NT // 2, 2, 16, N), F32),
         vmem((8 * N, 4 * N), F32),
         vmem((2, 8 * N, 4 * N), BF16),
         vmem((2, NT // 2, 2, 16, N), F32),
@@ -470,14 +491,14 @@
     ]
     for sizes in ((NC, 8, 4), (NC, NT)):
         scratch += [vmem((len(sizes), 8, N), F32)] + [vmem((n, 8, N), F32) for n in sizes]
-    scratch += [dma((n,)) for n in (5, 4, 3, 3)] + [dma(())] * 8
-    scratch += [dma((3,))] * 2 + [dma((2,))] * 6 + [dma((3,))] * 5
+    scratch += [dma((n,)) if n else dma(()) for n in (5, 5, 6, 6, 2, 2, 0, 0, 2, 2, 0, 0, 3, 3, 2, 2, 2, 2, 2, 2)]
+    scratch += [dma((3,))] * 5
     step = jax.ShapeDtypeStruct((1, 1, 1, N), F32)
     normal, alpha, beta = pl.pallas_call(
         kernel,
         out_shape=(jax.ShapeDtypeStruct(shard, F32), step, step),
         in_specs=[HBM] * 4 + [SMEM] * 2 + [HBM],
-        out_specs=(HBM, HBM, HBM),
+        out_specs=(pl.BlockSpec(memory_space=pl.ANY), pl.BlockSpec(memory_space=pl.ANY), pl.BlockSpec(memory_space=pl.ANY)),
         scratch_shapes=scratch,
         compiler_params=pltpu.CompilerParams(
             collective_id=0, has_side_effects=True, vmem_limit_bytes=60 * 2**20

time: 70.1 us -> 69.9 us (level)
  no operation moved by 1% of the time
where the time goes in v4:
time: 69.9 us; the launch traced here: 69.7 us
  Pallas kernels  66.9 us (96%)
  other arithmetic  1.53 us (2%)
  between operations  0.7 us (1%)
    pallas_call x1, Pallas kernels, shards(): pl.pallas_call(kernel, out_shape=(jax.ShapeDtypeStruct(shard, F32), step,...  66.9 us
    add x1, other arithmetic, shards(): next_p = next_r + beta * image_p  1.53 us

profile of v4, /device:TPU:1, one launch (start us, length us, event | category | flops | bytes accessed | tf_op | source)
XLA Modules:
  0.0 69.7 jit_solution(4396718085951889648)
XLA Ops:
  0.6 0.0 copy-start
  0.6 0.0 copy-start.1
  0.7 0.0 copy-start.2
  0.7 66.9 %shard_map.103 = (f32[2,4,16,128]{3,2,1,0:T(8,128)}, f32[1,1,1,128]{3,2,1,0:T(1,128)}, f32[1,1,1,128]{3,2,1,0:T(1,128)}) custom-call(f32[2,4,16,128]{3,2,1,0:T(8,128)} %p_hbm.1, f32[2,4,16,128]{3,2,1,0:T(8,128)} %r_hbm.1, f32[1,2,4,128,128]{4,3,2,1,0:T(8,128)} %s_hbm.1, f32[384,128]{1,0:T(8,128)} %bitcast.4, s32[32]{0:T(128)} %own.1, ...), custom_call_target="tpu_custom_call" | custom-call | tf_op jit(solution)/shard_map/pallas_call | solution.py:497
  67.5 0.0 copy-start.3
  67.5 0.0 copy-start.4
  67.6 0.0 copy-done
  67.6 0.0 copy-done.1
  67.6 0.0 copy-done.2
  67.6 0.6 copy-done.3
  68.2 0.1 copy-done.4
  68.2 1.5 %multiply_add_fusion = (f32[2,4,16,128]{3,2,1,0:T(8,128)}, f32[2,4,16,128]{3,2,1,0:T(8,128)}, f32[2,4,16,128]{3,2,1,0:T(8,128)}) fusion(f32[2,4,16,128]{3,2,1,0:T(8,128)S(1)} %copy-done, f32[128]{0:T(128)S(1)} %bitcast.7, f32[2,4,16,128]{3,2,1,0:T(8,128)S(1)} %copy-done.1, f32[2,4,16,128]{3,2,1,0:T(8,128)} %get-tuple-element.7, f32[128]{0:T(128)S(1)} %bitcast.6, ...), kind=kLoop, calls=%fused_computation | loop fusion | flops 98304 | bytes 459776 | tf_op jit(solution)/shard_map/add | solution.py:512
Async XLA Ops:
  0.6 66.9 %copy-start = (f32[2,4,16,128]{3,2,1,0:T(8,128)S(1)}, f32[2,4,16,128]{3,2,1,0:T(8,128)}, u32[]{:S(2)}) copy-start(f32[2,4,16,128]{3,2,1,0:T(8,128)} %p_hbm.1) | copy-start | bytes 196612
  0.6 66.9 %copy-start.1 = (f32[2,4,16,128]{3,2,1,0:T(8,128)S(1)}, f32[2,4,16,128]{3,2,1,0:T(8,128)}, u32[]{:S(2)}) copy-start(f32[2,4,16,128]{3,2,1,0:T(8,128)} %r_hbm.1) | copy-start | bytes 196612
  0.7 66.9 %copy-start.2 = (f32[2,4,16,128]{3,2,1,0:T(8,128)S(1)}, f32[2,4,16,128]{3,2,1,0:T(8,128)}, u32[]{:S(2)}) copy-start(f32[2,4,16,128]{3,2,1,0:T(8,128)} %param.9) | copy-start | bytes 196612
  67.5 0.6 copy-start.3
  67.5 0.7 copy-start.4
